TPU v7x, 256 devices: a whole 4x4x8 slice. The times are simulated.
256 devices in a mesh: grp: 64 (over y, z, core), dir: 4 (over x).
Axes of the slice: x: 4, y: 4, z: 8, core: 2. Of those that a mesh axis runs over, the one named last changes fastest.
Arguments:
- currents: bfloat16 [16384, 128], P('grp'), may hold values from -6 to 6
- basis_group: int32 [16384], P('grp'), may hold values from 0 to 1
- projection: bfloat16 [16384, 1024], P('grp', 'dir'), may hold values from -0.5 to 0.5
- filters: bfloat16 [4, 64, 1024], P(None, None, 'dir'), may hold values from -0.09375 to 0.09375
- pair_src: int32 [8192], P('grp'), may hold values from 0 to 63, as said below
- pair_dst: int32 [8192], P('grp'), may hold values from 0 to 63, as said below
- pair_type: int32 [8192], P('grp'), may hold values from 0 to 3
- live_count: int32 [64], P('grp'), may hold values from 64 to 128, as said below
- send_group: int32 [64, 64], replicated, may hold values from 0 to 1, as said below
- recv_group: int32 [64, 64], replicated, may hold values from 0 to 1, as said below
Outputs:
- field: bfloat16 [16384, 128], P('grp')
Inputs may be any that keep to these rules, and one draw needn't show every extreme that they name: `pair_src`: for each reader, its first 64 slots name every owner once. `pair_dst`: for each reader, its first 64 slots name every owner once. `live_count`: some reader has all 128 slots live. `send_group`: each row names every one of the owner's groups at least once. `recv_group`: each row names every one of the owner's groups at least once.
All inputs are finite; a program needn't handle non-finite values.
Results may differ from a plain program's by a relative error of at most 0.0058.
Values may be sent and summed in bfloat16 or wider, within the bound.
A program may use at most 192 MiB of HBM per device.

v0:
```python
import math

import jax
import jax.numpy as jnp
from jax import lax
from jax.sharding import PartitionSpec as P

TAPS = 64
G_DEV = 2
TYPES = 4


def local(
    currents,
    basis_group,
    projection,
    filters,
    pair_src,
    pair_dst,
    pair_type,
    live_count,
    send_group,
    recv_group,
):
    readers = lax.axis_size("grp")
    position = lax.axis_index("grp")
    steps = currents.shape[1]
    width = projection.shape[1]
    slots = pair_src.shape[0]
    labels = jnp.arange(G_DEV, dtype=jnp.int32)
    member = (basis_group[:, None] == labels[None, :]).astype(jnp.bfloat16)
    spread = currents[:, None, :] * member[:, :, None]
    signature = jnp.einsum(
        "bk,bgt->gkt", projection, spread, preferred_element_type=jnp.float32
    ).astype(jnp.bfloat16)
    everything = lax.all_gather(signature, "grp", axis=0, tiled=True)
    chosen = pair_src * G_DEV + send_group[pair_src, position]
    pair_signal = jnp.take(everything, chosen, axis=0)
    live = jnp.arange(slots, dtype=jnp.int32) < live_count[0]
    bucket_index = pair_dst * TYPES + pair_type
    bucket_select_mask = (
        (jnp.arange(readers * TYPES, dtype=jnp.int32)[:, None] == bucket_index[None, :])
        & live[None, :]
    ).astype(jnp.bfloat16)
    times = jnp.arange(steps, dtype=jnp.int32)
    taps_index = jnp.arange(TAPS, dtype=jnp.int32)
    shifter = (times[None, None, :] - times[None, :, None] == taps_index[:, None, None]).astype(
        jnp.bfloat16
    )
    toeplitz = jnp.einsum(
        "cuk,ust->kcst", filters, shifter, preferred_element_type=jnp.float32
    ).astype(jnp.bfloat16)
    block = math.gcd(width, 64)

    def translate(index, partial_value):
        start = index * block
        signal_tile_block = lax.dynamic_slice_in_dim(pair_signal, start, block, 1)
        gathered = jnp.einsum(
            "ay,ydi->adi", bucket_select_mask, signal_tile_block, preferred_element_type=jnp.float32
        )
        gathered = gathered.reshape(readers, TYPES, block, steps)
        taps_block = lax.dynamic_slice_in_dim(toeplitz, start, block, 0).astype(jnp.float32)
        summed = jnp.einsum("dcks,kcst->dkt", gathered, taps_block, precision=lax.Precision.HIGHEST)
        return lax.dynamic_update_slice_in_dim(partial_value, summed, start, 1)

    partial_value = lax.fori_loop(
        0, width // block, translate, jnp.zeros((readers, width, steps), dtype=jnp.float32)
    )
    received = lax.all_to_all(partial_value, "grp", split_axis=0, concat_axis=0, tiled=True)
    self_received = lax.dynamic_index_in_dim(recv_group, position, 0, keepdims=False)
    owner_mask = (labels[:, None] == self_received[None, :]).astype(jnp.float32)
    incoming = jnp.einsum(
        "gr,rkt->gkt", owner_mask, received, precision=lax.Precision.HIGHEST
    ).astype(jnp.bfloat16)
    spread_field = jnp.einsum(
        "bk,gkt->bgt", projection, incoming, preferred_element_type=jnp.float32
    )
    field_terms = jnp.sum(spread_field * member.astype(jnp.float32)[:, :, None], axis=1)
    return lax.psum(field_terms, "dir").astype(jnp.bfloat16)


def solution(mesh):
    return jax.shard_map(
        local,
        mesh=mesh,
        in_specs=(
            P("grp", None),
            P("grp"),
            P("grp", "dir"),
            P(None, None, "dir"),
            P("grp"),
            P("grp"),
            P("grp"),
            P("grp"),
            P(),
            P(),
        ),
        out_specs=P("grp", None),
        check_vma=False,
    )
```

profile of v0, /device:TPU:1, one launch (start us, length us, event | category | flops | bytes accessed | tf_op | source)
XLA Modules:
  0.0 480.0 jit_solution(2588424089395567460)
XLA Ops:
  6.5 0.0 copy-start
  6.5 0.0 all-gather.2.cloned.1.call-start
  6.5 0.7 fusion.43
  7.3 0.9 copy.19
  8.2 1.1 fusion.28
  9.3 0.8 copy.20
  10.1 0.0 all-gather.2.cloned.1.call-update
  10.1 0.0 copy-done
  10.1 14.5 %convert_bitcast_fusion = bf16[256,4,128,128]{0,3,1,2:T(8,128)(2,1)} fusion(s32[128,128]{1,0:T(8,128)S(1)} %iota_subtract_fusion, bf16[4,64,256]{2,1,0:T(8,128)(2,1)S(1)} %copy-done), kind=kOutput, calls=%fused_computation.18 | convolution fusion | flops 2165309440 | bytes 33751040 | tf_op jit(solution)/shard_map/cuk,ust->kcst/dot_general | solution.py:50
  24.6 46.3 %copy.21 = bf16[256,4,128,128]{3,2,1,0:T(8,128)(2,1)} copy(bf16[256,4,128,128]{0,3,1,2:T(8,128)(2,1)} %convert_bitcast_fusion) | data formatting | bytes 67108864
  71.6 0.0 copy-done.4
  71.6 0.0 copy-done.2
  71.6 1.3 gather_fusion
  72.9 0.0 copy-done.5
  72.9 24.6 %all-gather.2.cloned.1.call-done = bf16[128,256,128]{2,1,0:T(8,128)(2,1)} async-done(((bf16[2,256,128]{2,1,0:T(8,128)(2,1)}), bf16[128,256,128]{2,1,0:T(8,128)(2,1)}) %all-gather.2.cloned.1.call-update) | async-done | bytes 8388624 | tf_op jit(solution)/shard_map/all_gather | solution.py:36
  97.5 9.9 %gather_fusion.1 = bf16[128,256,128]{2,1,0:T(8,128)(2,1)} fusion(bf16[128,256,128]{2,1,0:T(8,128)(2,1)} %all-gather.2.cloned.1.call-done, s32[1024]{0:T(1024)S(1)} %pad_clamp_fusion), kind=kCustom, calls=%fused_computation.1 | custom fusion | bytes 16777728 | tf_op jit(solution)/shard_map/jit(_take)/gather | solution.py:38
  107.5 7.4 %broadcast_select_fusion = bf16[128,256,128]{2,1,0:T(8,128)(2,1)} fusion(bf16[128,256,128]{2,1,0:T(8,128)(2,1)} %gather_fusion.1, pred[128]{0:T(512)(128)(4,1)S(1)} %get-tuple-element.140), kind=kLoop, calls=%fused_computation.21 | loop fusion | flops 4194304 | bytes 16777344 | tf_op jit(solution)/shard_map/jit(_take)/select_n | solution.py:38
  114.9 4.2 broadcast_in_dim.16.clone
  119.1 135.3 %while.14 = (s32[]{:T(128)}, f32[64,256,128]{2,1,0:T(8,128)}, bf16[256,4,128,128]{3,2,1,0:T(8,128)(2,1)}, bf16[128,256,128]{2,1,0:T(8,128)(2,1)}, s32[128]{0:T(1...) while((s32[]{:T(128)}, f32[64,256,128]{2,1,0:T(8,128)}, ...), condition=%wide.region_1.2_spmd.clone, body=%wide.region_0.1_spmd.clone.sunk | while | flops 3758194688 | bytes 54526756 | solution.py:66
  119.1 1.8 constant_dynamic-slice_fusion.2
  120.9 6.3 %convolution_bitcast_fusion.3 = f32[256,64,128]{0,2,1:T(8,128)} fusion(bf16[128,64,128]{2,1,0:T(8,128)(2,1)S(1)} %constant_dynamic-slice_fusion.2, s32[128]{0:T(128)S(1)} %get-tuple-element.205, pred[128]{0:T(512)(128)(4,1)S(1)} %get-tuple-element.206), kind=kOutput, calls=%fused_computation.6.clone.1 | convolution fusion | flops 536969216 | bytes 10486400 | tf_op jit(solution)/shard_map/while/body/eval_jaxpr/ay,ydi->adi/dot_general | solution.py:58
  127.2 8.7 %copy.53 = f32[256,64,128]{2,1,0:T(8,128)} copy(f32[256,64,128]{0,2,1:T(8,128)} %convolution_bitcast_fusion.3) | data formatting | bytes 16777216 | tf_op jit(solution)/shard_map/while/body/eval_jaxpr/ay,ydi->adi/dot_general | solution.py:58
  135.9 14.5 %fusion.53 = f32[64,64,128]{2,0,1:T(8,128)S(1)} fusion(f32[64,4,64,128]{3,2,1,0:T(8,128)} %bitcast.49, bf16[256,4,128,128]{3,2,1,0:T(8,128)(2,1)} %get-tuple-element.203, s32[]{:T(128)S(6)} %select_n.42), kind=kOutput, calls=%fused_computation.9.clone.1 | convolution fusion | flops 3221225472 | bytes 18874372 | tf_op jit(solution)/shard_map/while/body/eval_jaxpr/dcks,kcst->dkt/dot_general | solution.py:63
  150.4 2.5 copy_dynamic-update-slice_fusion.2
  152.9 1.8 constant_dynamic-slice_fusion.2
  154.7 6.3 %convolution_bitcast_fusion.3 = f32[256,64,128]{0,2,1:T(8,128)} fusion(bf16[128,64,128]{2,1,0:T(8,128)(2,1)S(1)} %constant_dynamic-slice_fusion.2, s32[128]{0:T(128)S(1)} %get-tuple-element.205, pred[128]{0:T(512)(128)(4,1)S(1)} %get-tuple-element.206), kind=kOutput, calls=%fused_computation.6.clone.1 | convolution fusion | flops 536969216 | bytes 10486400 | tf_op jit(solution)/shard_map/while/body/eval_jaxpr/ay,ydi->adi/dot_general | solution.py:58
  161.0 8.7 %copy.53 = f32[256,64,128]{2,1,0:T(8,128)} copy(f32[256,64,128]{0,2,1:T(8,128)} %convolution_bitcast_fusion.3) | data formatting | bytes 16777216 | tf_op jit(solution)/shard_map/while/body/eval_jaxpr/ay,ydi->adi/dot_general | solution.py:58
  169.8 14.5 %fusion.53 = f32[64,64,128]{2,0,1:T(8,128)S(1)} fusion(f32[64,4,64,128]{3,2,1,0:T(8,128)} %bitcast.49, bf16[256,4,128,128]{3,2,1,0:T(8,128)(2,1)} %get-tuple-element.203, s32[]{:T(128)S(6)} %select_n.42), kind=kOutput, calls=%fused_computation.9.clone.1 | convolution fusion | flops 3221225472 | bytes 18874372 | tf_op jit(solution)/shard_map/while/body/eval_jaxpr/dcks,kcst->dkt/dot_general | solution.py:63
  184.2 2.5 copy_dynamic-update-slice_fusion.2
  186.7 1.8 constant_dynamic-slice_fusion.2
  188.5 6.3 %convolution_bitcast_fusion.3 = f32[256,64,128]{0,2,1:T(8,128)} fusion(bf16[128,64,128]{2,1,0:T(8,128)(2,1)S(1)} %constant_dynamic-slice_fusion.2, s32[128]{0:T(128)S(1)} %get-tuple-element.205, pred[128]{0:T(512)(128)(4,1)S(1)} %get-tuple-element.206), kind=kOutput, calls=%fused_computation.6.clone.1 | convolution fusion | flops 536969216 | bytes 10486400 | tf_op jit(solution)/shard_map/while/body/eval_jaxpr/ay,ydi->adi/dot_general | solution.py:58
  194.8 8.7 %copy.53 = f32[256,64,128]{2,1,0:T(8,128)} copy(f32[256,64,128]{0,2,1:T(8,128)} %convolution_bitcast_fusion.3) | data formatting | bytes 16777216 | tf_op jit(solution)/shard_map/while/body/eval_jaxpr/ay,ydi->adi/dot_general | solution.py:58
  203.6 14.5 %fusion.53 = f32[64,64,128]{2,0,1:T(8,128)S(1)} fusion(f32[64,4,64,128]{3,2,1,0:T(8,128)} %bitcast.49, bf16[256,4,128,128]{3,2,1,0:T(8,128)(2,1)} %get-tuple-element.203, s32[]{:T(128)S(6)} %select_n.42), kind=kOutput, calls=%fused_computation.9.clone.1 | convolution fusion | flops 3221225472 | bytes 18874372 | tf_op jit(solution)/shard_map/while/body/eval_jaxpr/dcks,kcst->dkt/dot_general | solution.py:63
  218.0 2.5 copy_dynamic-update-slice_fusion.2
  220.6 1.8 constant_dynamic-slice_fusion.2
  222.3 6.3 %convolution_bitcast_fusion.3 = f32[256,64,128]{0,2,1:T(8,128)} fusion(bf16[128,64,128]{2,1,0:T(8,128)(2,1)S(1)} %constant_dynamic-slice_fusion.2, s32[128]{0:T(128)S(1)} %get-tuple-element.205, pred[128]{0:T(512)(128)(4,1)S(1)} %get-tuple-element.206), kind=kOutput, calls=%fused_computation.6.clone.1 | convolution fusion | flops 536969216 | bytes 10486400 | tf_op jit(solution)/shard_map/while/body/eval_jaxpr/ay,ydi->adi/dot_general | solution.py:58
  228.7 8.7 %copy.53 = f32[256,64,128]{2,1,0:T(8,128)} copy(f32[256,64,128]{0,2,1:T(8,128)} %convolution_bitcast_fusion.3) | data formatting | bytes 16777216 | tf_op jit(solution)/shard_map/while/body/eval_jaxpr/ay,ydi->adi/dot_general | solution.py:58
  237.4 14.5 %fusion.53 = f32[64,64,128]{2,0,1:T(8,128)S(1)} fusion(f32[64,4,64,128]{3,2,1,0:T(8,128)} %bitcast.49, bf16[256,4,128,128]{3,2,1,0:T(8,128)(2,1)} %get-tuple-element.203, s32[]{:T(128)S(6)} %select_n.42), kind=kOutput, calls=%fused_computation.9.clone.1 | convolution fusion | flops 3221225472 | bytes 18874372 | tf_op jit(solution)/shard_map/while/body/eval_jaxpr/dcks,kcst->dkt/dot_general | solution.py:63
  251.9 2.5 copy_dynamic-update-slice_fusion.2
  254.4 6.4 %all-to-all-start = ((f32[64,256,128]{2,1,0:T(8,128)}), f32[64,256,128]{2,1,0:T(8,128)}, u32[]{:S(2)}, u32[]{:S(2)}) async-start(f32[64,256,128]{2,1,0:T(8,128)} %get-tuple-element.99), calls=%async_computation | async-start | bytes 16777216 | tf_op jit(solution)/shard_map/all_to_all | solution.py:69
  260.9 0.0 copy-start.3
  260.9 0.0 copy-start.1
  260.9 0.7 dynamic-slice_bitcast_fusion
  261.6 185.0 %all-to-all-done = f32[64,256,128]{2,1,0:T(8,128)} async-done(((f32[64,256,128]{2,1,0:T(8,128)}), f32[64,256,128]{2,1,0:T(8,128)}, u32[]{:S(2)}, u32[]{:S(2)}) %all-to-all-start) | async-done | bytes 8388640 | tf_op jit(solution)/shard_map/all_to_all | solution.py:69
  446.6 10.4 %fusion.25 = bf16[2,256,128]{2,0,1:T(2,128)(2,1)S(1)} fusion(f32[64,256,128]{2,1,0:T(8,128)} %all-to-all-done, s32[64]{0:T(128)S(1)} %dynamic-slice_bitcast_fusion), kind=kOutput, calls=%fused_computation.29 | convolution fusion | flops 50397312 | bytes 8519936 | tf_op jit(solution)/shard_map/gr,rkt->gkt/dot_general | solution.py:72
  457.0 0.2 fusion.24
  457.3 15.1 %all-reduce.2 = bf16[256,128]{0,1:T(8,128)(2,1)S(1)} all-reduce(f32[256,128]{0,1:T(8,128)S(1)} %fusion.24), channel_id=1, replica_groups=mesh['grp'=64,'dir'=4] {'dir'}, use_global_device_ids=true, to_apply=%region_3.4 | all-reduce | flops 32768 | bytes 196608 | tf_op jit(solution)/shard_map/psum | solution.py:79
  472.4 0.7 copy.26
  (13 shorter events, 0.1 us)
Async XLA Ops:
  6.5 3.6 copy-start
  6.5 91.0 %all-gather.2.cloned.1.call-start = ((), (), s32[]{:S(2)}) async-start(), calls=%async_computation.1 | async-start | bytes 8519680 | tf_op jit(solution)/shard_map/all_gather | solution.py:36
  24.6 47.0 %copy-start.4 = (s32[128]{0:T(128)S(1)}, s32[128]{0:T(128)}, u32[]{:S(2)}) copy-start(s32[128]{0:T(128)} %param.16) | copy-start | bytes 1540
  24.6 47.0 %copy-start.2 = (s32[64,64]{1,0:T(8,128)S(1)}, s32[64,64]{1,0:T(8,128)}, u32[]{:S(2)}) copy-start(s32[64,64]{1,0:T(8,128)} %param.20) | copy-start | bytes 49156
  24.6 48.3 %copy-start.5 = (s32[128]{0:T(128)S(1)}, s32[128]{0:T(128)}, u32[]{:S(2)}) copy-start(s32[128]{0:T(128)} %param.18) | copy-start | bytes 1540
  24.6 48.3 %copy-start.6 = (s32[128]{0:T(128)S(1)}, s32[128]{0:T(128)}, u32[]{:S(2)}) copy-start(s32[128]{0:T(128)} %param.17) | copy-start | bytes 1540
  254.4 192.2 %all-to-all-start = ((f32[64,256,128]{2,1,0:T(8,128)}), f32[64,256,128]{2,1,0:T(8,128)}, u32[]{:S(2)}, u32[]{:S(2)}) async-start(f32[64,256,128]{2,1,0:T(8,128)} %get-tuple-element.99), calls=%async_computation | async-start | bytes 16777216 | tf_op jit(solution)/shard_map/all_to_all | solution.py:69
  260.9 196.2 %copy-start.3 = (bf16[256,256]{1,0:T(8,128)(2,1)S(1)}, bf16[256,256]{1,0:T(8,128)(2,1)}, u32[]{:S(2)}) copy-start(bf16[256,256]{1,0:T(8,128)(2,1)} %param.14) | copy-start | bytes 393220
  260.9 212.3 %copy-start.1 = (bf16[4,64,256]{2,1,0:T(8,128)(2,1)S(1)}, bf16[4,64,256]{2,1,0:T(8,128)(2,1)}, u32[]{:S(2)}) copy-start(bf16[4,64,256]{2,1,0:T(8,128)(2,1)} %param.15) | copy-start | bytes 393220
Sparse Core Ops, SparseCore 0:
  10.2 87.2 all-gather.1
where the time goes:
time: 483 us; the launch traced here: 480 us
  waiting for transfers between devices  210 us (43%)
  local copies, waits for them, and re-layouts  117 us (24%)
  matrix products  109 us (23%)
  blocking collectives  15.1 us (3%)
  between operations  14.2 us (3%)
  other arithmetic  8.18 us (2%)
  starting transfers between devices  6.44 us (1%)
    all_to_all x1, waiting for transfers between devices, local(): lax.all_to_all(partial_value, 'grp', split_axis=0, concat_axis=0, tiled=T...  185 us
    dot_general x4, matrix products, translate(): jnp.einsum('dcks,kcst->dkt', gathered, taps_block, precision=lax.Precisio...  57.9 us
    unnamed x16, local copies, waits for them, and re-layouts  47.3 us
    dot_general x4, local copies, waits for them, and re-layouts, translate(): jnp.einsum('ay,ydi->adi', bucket_select_mask, signal_tile_block, preferre...  34.9 us
    dot_general x4, matrix products, translate(): jnp.einsum('ay,ydi->adi', bucket_select_mask, signal_tile_block, preferre...  25.3 us
    all_gather x1, waiting for transfers between devices, local(): everything = lax.all_gather(signature, 'grp', axis=0, tiled=True)  24.6 us
    psum x1, blocking collectives, local(): return lax.psum(field_terms, 'dir').astype(jnp.bfloat16)  15.1 us
    dot_general x1, matrix products, local(): jnp.einsum('cuk,ust->kcst', filters, shifter, preferred_element_type=jnp....  14.5 us
  transfers between devices with their start and end apart: 2, of which 2 were waited for; matrix products, arithmetic and copies ran while one was open for 13% of the time, Pallas kernels for 0%

commit v1 on v0

v1 whole, which is shorter than its diff:
```python
import functools

import jax
import jax.numpy as jnp
from jax import lax
from jax.experimental import pallas as pl
from jax.experimental.pallas import tpu as pltpu
from jax.sharding import PartitionSpec as P

MESH = pl.DeviceIdType.MESH
F32 = jnp.float32
BF16 = jnp.bfloat16
TYPES = 4
GROUPS_OWN = 2
KD = 4
NTAB = 8
READER_CHUNK = 8


def dot_nt(a, b):
    return lax.dot_general(a, b, (((1,), (1,)), ((), ())), preferred_element_type=F32)


def dot(a, b):
    return jnp.dot(a, b, preferred_element_type=F32)


def iota(shape, axis):
    return lax.broadcasted_iota(jnp.int32, shape, axis)


def kernel(
    n,
    nd,
    taps,
    cur_h,
    bg_h,
    proj_h,
    filt_h,
    src_h,
    dst_h,
    typ_h,
    live_h,
    sg_h,
    rg_h,
    out_h,
    cur,
    bg,
    proj,
    filt,
    src,
    dst,
    typ,
    live,
    sg,
    rg,
    local_sems,
    tab_send,
    tab_recv,
    sig_send,
    sig_recv,
    in_send,
    in_recv,
    term_send,
    term_recv,
    fin_send,
    send_sems,
    recv_sems,
    out_sem,
    pattern,
    back,
    toep,
    index_b,
    index_s,
    rows_f,
):
    p = lax.axis_index("grp")
    d = lax.axis_index("dir")
    rows, steps = cur.shape
    slots = src.shape[1]
    groups = GROUPS_OWN * n
    share = rows // nd

    locals_ = []
    for i, (a, b) in enumerate(
        [
            (src_h, src),
            (dst_h, dst),
            (typ_h, typ),
            (live_h, live),
            (sg_h, sg),
            (rg_h, rg),
            (proj_h, proj),
            (cur_h, cur),
            (bg_h, bg),
            (filt_h, filt),
        ]
    ):
        copy = pltpu.make_async_copy(a, b, local_sems.at[i])
        copy.start()
        locals_.append(copy)

    barrier = pltpu.get_barrier_semaphore()

    def greet(i, carry):
        pl.semaphore_signal(barrier, 1, device_id=(lax.rem(p + i, n), d), device_id_type=MESH)
        return carry

    lax.fori_loop(1, n, greet, 0)
    for i in range(1, nd):
        pl.semaphore_signal(barrier, 1, device_id=(p, lax.rem(d + i, nd)), device_id_type=MESH)

    for copy in locals_[:6]:
        copy.wait()
    owners = iota((n, slots), 0)
    here = iota((n, n), 1) == p
    send_col = jnp.sum(jnp.where(here, sg[...].astype(F32), 0.0), axis=1, keepdims=True)
    recv_col = jnp.sum(jnp.where(here, rg[...].astype(F32), 0.0), axis=1, keepdims=True)
    send_of = jnp.sum(jnp.where(owners == src[...], send_col, 0.0), axis=0, keepdims=True)
    recv_of = jnp.sum(jnp.where(owners == dst[...], recv_col, 0.0), axis=0, keepdims=True)
    source = send_of * n + src[...].astype(F32)
    target = recv_of * n + dst[...].astype(F32)
    is_live = jnp.where(iota((1, slots), 1) < live[...], 1.0, 0.0)
    row = iota((NTAB, slots), 0)
    table = jnp.where(
        row == 0,
        source,
        jnp.where(
            row == 1, target, jnp.where(row == 2, typ[...].astype(F32), jnp.where(row == 3, is_live, 0.0))
        ),
    )
    tab_send[...] = table.astype(BF16)
    tab_recv[pl.ds(p, 1)] = table.astype(BF16)[None]

    for copy in locals_[6:9]:
        copy.wait()
    width = proj.shape[1]
    pick = (iota((GROUPS_OWN * width, width), 0) // GROUPS_OWN == iota((GROUPS_OWN * width, width), 1))
    spread = dot_nt(pick.astype(F32).astype(BF16), proj[...])
    owned = lax.rem(iota((GROUPS_OWN * width, rows), 0), GROUPS_OWN) == bg[...]
    pattern[...] = jnp.where(owned, spread, 0.0).astype(BF16)
    signature = dot(pattern[...], cur[...])
    sig_send[...] = signature.reshape(n, GROUPS_OWN * KD, steps).astype(BF16)
    sig_recv[pl.ds(p, 1)] = sig_send[pl.ds(p, 1)]

    pl.semaphore_wait(barrier, n - 1 + nd - 1)

    def send_table(i, carry):
        peer = lax.rem(p + i, n)
        pltpu.make_async_remote_copy(
            src_ref=tab_send,
            dst_ref=tab_recv.at[p],
            send_sem=send_sems.at[0],
            recv_sem=recv_sems.at[0],
            device_id=(peer, d),
            device_id_type=MESH,
        ).start()
        return carry

    def send_signature(i, carry):
        peer = lax.rem(p + i, n)
        pltpu.make_async_remote_copy(
            src_ref=sig_send.at[peer],
            dst_ref=sig_recv.at[p],
            send_sem=send_sems.at[1],
            recv_sem=recv_sems.at[1],
            device_id=(peer, d),
            device_id_type=MESH,
        ).start()
        return carry

    lax.fori_loop(1, n, send_table, 0)
    lax.fori_loop(1, n, send_signature, 0)

    def await_bytes(ref, sem):
        pltpu.make_async_copy(ref, ref, sem).wait()

    eye = (iota((rows, rows), 0) == iota((rows, rows), 1)).astype(F32).astype(BF16)
    back[...] = dot_nt(eye, pattern[...]).astype(BF16)
    locals_[9].wait()
    mine = (iota((8, width), 1) == iota((8, width), 0) + KD * p) & (iota((8, width), 0) < KD)
    tap_rows = dot_nt(mine.astype(F32).astype(BF16), filt[...])
    lag = iota((steps, steps), 1) - iota((steps, steps), 0)
    causal = (lag >= 0) & (lag < taps)
    for k in range(KD):
        for c in range(TYPES):
            first = c * taps
            base = first // steps * steps
            line = jnp.broadcast_to(tap_rows[k : k + 1, base : base + steps], (steps, steps))
            turned = pltpu.roll(line, (steps - (first - base)) % steps, 1, stride=1, stride_axis=0)
            toep[k, c * steps : (c + 1) * steps, :] = jnp.where(causal, turned, 0.0).astype(BF16)

    await_bytes(tab_recv.at[pl.ds(0, n - 1)], recv_sems.at[0])
    tables = tab_recv[...].astype(F32)
    kind = tables[:, 2, :]
    high = jnp.where(kind >= 2.0, 1.0, 0.0)
    index_b[...] = jnp.where(tables[:, 3, :] > 0.0, high * groups + tables[:, 1, :], -1.0)
    index_s[...] = (kind - 2.0 * high) * groups + tables[:, 0, :]
    wide = iota((2 * groups, slots), 0).astype(F32)

    def count_readers(step, total):
        hot_b, hot_s = [], []
        for j in range(READER_CHUNK):
            r = step * READER_CHUNK + j
            hot_b.append(jnp.where(wide == index_b[pl.ds(r, 1), :], 1.0, 0.0).astype(BF16))
            hot_s.append(jnp.where(wide == index_s[pl.ds(r, 1), :], 1.0, 0.0).astype(BF16))
        return total + dot_nt(jnp.concatenate(hot_b, axis=1), jnp.concatenate(hot_s, axis=1))

    count = lax.fori_loop(
        0, n // READER_CHUNK, count_readers, jnp.zeros((2 * groups, 2 * groups), F32)
    )
    hundreds = jnp.floor(count * (1.0 / 256.0))
    units = count - 256.0 * hundreds
    parts = []
    for c in range(TYPES):
        r0, c0 = c // 2 * groups, c % 2 * groups
        parts.append(
            jnp.concatenate(
                [
                    units[r0 : r0 + groups, c0 : c0 + groups],
                    hundreds[r0 : r0 + groups, c0 : c0 + groups],
                ],
                axis=1,
            )
        )
    counts = jnp.concatenate(parts, axis=0).astype(BF16)

    await_bytes(sig_recv.at[pl.ds(0, n - 1)], recv_sems.at[1])
    rows_f[...] = sig_recv[...].astype(F32)
    by_k = []
    for k in range(KD):
        by_k.append(
            jnp.concatenate([rows_f[:, GROUPS_OWN * k + g, :] for g in range(GROUPS_OWN)], axis=0)
        )
    signal = jnp.concatenate(by_k, axis=1)
    signal = jnp.concatenate([signal, 256.0 * signal], axis=0).astype(BF16)
    summed = dot(counts, signal)
    for k in range(KD):
        part = summed[:, k * steps : (k + 1) * steps]
        part = jnp.concatenate([part[c * groups : (c + 1) * groups] for c in range(TYPES)], axis=1)
        upper = part.astype(BF16)
        lower = (part - upper.astype(F32)).astype(BF16)
        both = dot(jnp.concatenate([upper, lower], axis=0), toep[k])
        arriving = both[:groups] + both[groups:]
        for g in range(GROUPS_OWN):
            rows_f[:, GROUPS_OWN * k + g, :] = arriving[g * n : (g + 1) * n]
    in_send[...] = rows_f[...].astype(BF16)
    in_recv[pl.ds(p, 1)] = in_send[pl.ds(p, 1)]

    def send_incoming(i, carry):
        peer = lax.rem(p + i, n)
        pltpu.make_async_remote_copy(
            src_ref=in_send.at[peer],
            dst_ref=in_recv.at[p],
            send_sem=send_sems.at[2],
            recv_sem=recv_sems.at[2],
            device_id=(peer, d),
            device_id_type=MESH,
        ).start()
        return carry

    lax.fori_loop(1, n, send_incoming, 0)
    await_bytes(in_recv.at[pl.ds(0, n - 1)], recv_sems.at[2])

    incoming = in_recv[...].astype(F32).reshape(n * GROUPS_OWN * KD, steps).astype(BF16)
    term_send[...] = dot(back[...], incoming).reshape(nd, share, steps)
    term_recv[pl.ds(d, 1)] = term_send[pl.ds(d, 1)]
    for i in range(1, nd):
        peer = lax.rem(d + i, nd)
        pltpu.make_async_remote_copy(
            src_ref=term_send.at[peer],
            dst_ref=term_recv.at[d],
            send_sem=send_sems.at[3],
            recv_sem=recv_sems.at[3],
            device_id=(p, peer),
            device_id_type=MESH,
        ).start()
    await_bytes(term_recv.at[pl.ds(0, nd - 1)], recv_sems.at[3])
    total = term_recv[0]
    for i in range(1, nd):
        total = total + term_recv[i]
    fin_send[...] = total.astype(BF16)
    own = pltpu.make_async_copy(fin_send, out_h.at[d], out_sem)
    own.start()
    for i in range(1, nd):
        peer = lax.rem(d + i, nd)
        pltpu.make_async_remote_copy(
            src_ref=fin_send,
            dst_ref=out_h.at[d],
            send_sem=send_sems.at[4],
            recv_sem=recv_sems.at[4],
            device_id=(p, peer),
            device_id_type=MESH,
        ).start()
    await_bytes(tab_recv.at[pl.ds(0, n - 1)], send_sems.at[0])
    await_bytes(sig_send.at[pl.ds(0, n - 1)], send_sems.at[1])
    await_bytes(in_send.at[pl.ds(0, n - 1)], send_sems.at[2])
    await_bytes(term_send.at[pl.ds(0, nd - 1)], send_sems.at[3])
    own.wait()
    await_bytes(out_h.at[pl.ds(0, nd - 1)], send_sems.at[4])
    await_bytes(out_h.at[pl.ds(0, nd - 1)], recv_sems.at[4])


def local(
    currents,
    basis_group,
    projection,
    filters,
    pair_src,
    pair_dst,
    pair_type,
    live_count,
    send_group,
    recv_group,
):
    n = lax.axis_size("grp")
    nd = lax.axis_size("dir")
    rows, steps = currents.shape
    width = projection.shape[1]
    taps = filters.shape[1]
    slots = pair_src.shape[0]
    groups = GROUPS_OWN * n
    msg = GROUPS_OWN * KD
    any_space = pl.BlockSpec(memory_space=pltpu.HBM)
    out = pl.pallas_call(
        functools.partial(kernel, n, nd, taps),
        out_shape=jax.ShapeDtypeStruct((nd, rows // nd, steps), BF16),
        in_specs=[any_space] * 10,
        out_specs=any_space,
        scratch_shapes=[
            pltpu.VMEM((rows, steps), BF16),
            pltpu.VMEM((1, rows), jnp.int32),
            pltpu.VMEM((rows, width), BF16),
            pltpu.VMEM((TYPES * taps, width), BF16),
            pltpu.VMEM((1, slots), jnp.int32),
            pltpu.VMEM((1, slots), jnp.int32),
            pltpu.VMEM((1, slots), jnp.int32),
            pltpu.VMEM((1, 1), jnp.int32),
            pltpu.VMEM((n, n), jnp.int32),
            pltpu.VMEM((n, n), jnp.int32),
            pltpu.SemaphoreType.DMA((10,)),
            pltpu.VMEM((NTAB, slots), BF16),
            pltpu.VMEM((n, NTAB, slots), BF16),
            pltpu.VMEM((n, msg, steps), BF16),
            pltpu.VMEM((n, msg, steps), BF16),
            pltpu.VMEM((n, msg, steps), BF16),
            pltpu.VMEM((n, msg, steps), BF16),
            pltpu.VMEM((nd, rows // nd, steps), F32),
            pltpu.VMEM((nd, rows // nd, steps), F32),
            pltpu.VMEM((rows // nd, steps), BF16),
            pltpu.SemaphoreType.DMA((5,)),
            pltpu.SemaphoreType.DMA((5,)),
            pltpu.SemaphoreType.DMA,
            pltpu.VMEM((GROUPS_OWN * width, rows), BF16),
            pltpu.VMEM((rows, GROUPS_OWN * width), BF16),
            pltpu.VMEM((KD, TYPES * steps, steps), BF16),
            pltpu.VMEM((n, slots), F32),
            pltpu.VMEM((n, slots), F32),
            pltpu.VMEM((n, msg, steps), F32),
        ],
        compiler_params=pltpu.CompilerParams(
            collective_id=0, has_side_effects=True, vmem_limit_bytes=32 * 1024 * 1024
        ),
        name="far_field",
    )(
        currents,
        basis_group.reshape(1, rows),
        projection,
        filters.reshape(TYPES * taps, width),
        pair_src.reshape(1, slots),
        pair_dst.reshape(1, slots),
        pair_type.reshape(1, slots),
        live_count.reshape(1, 1),
        send_group,
        recv_group,
    )
    return out.reshape(rows, steps)


def solution(mesh):
    return jax.shard_map(
        local,
        mesh=mesh,
        in_specs=(
            P("grp", None),
            P("grp"),
            P("grp", "dir"),
            P(None, None, "dir"),
            P("grp"),
            P("grp"),
            P("grp"),
            P("grp"),
            P(),
            P(),
        ),
        out_specs=P("grp", None),
        check_vma=False,
    )
```

time: 483 us -> 44 us (0.09)
  waiting for transfers between devices: 210 us -> 0 us
  local copies, waits for them, and re-layouts: 117 us -> 5.47 us
  matrix products: 109 us -> 0 us
  Pallas kernels: 0 us -> 37.6 us
  blocking collectives: 15.1 us -> 0 us
  between operations: 14.2 us -> 0.7 us
  other arithmetic: 8.18 us -> 0 us
  starting transfers between devices: 6.44 us -> 0 us
    all_to_all x1 -> x0, waiting for transfers between devices: 185 us -> none  [local(): lax.all_to_all(partial_value, 'grp', split_axis=0, concat_axis=0, tiled=T...]
    dot_general x12 -> x0, matrix products: 109 us -> none  [the longest x4 57.9 us: translate(): jnp.einsum('dcks,kcst->dkt', gathered, taps_block, precision=lax.Precisio...]
    unnamed x16 -> x19, local copies, waits for them, and re-layouts: 47.3 us -> 5.47 us
    pallas_call x0 -> x1, Pallas kernels: none -> 37.6 us  [local(): pl.pallas_call(functools.partial(kernel, n, nd, taps), out_shape=jax.Shap...]
    dot_general x4 -> x0, local copies, waits for them, and re-layouts: 34.9 us -> none  [translate(): jnp.einsum('ay,ydi->adi', bucket_select_mask, signal_tile_block, preferre...]
    all_gather x1 -> x0, waiting for transfers between devices: 24.6 us -> none  [local(): everything = lax.all_gather(signature, 'grp', axis=0, tiled=True)]
    psum x1 -> x0, blocking collectives: 15.1 us -> none  [local(): return lax.psum(field_terms, 'dir').astype(jnp.bfloat16)]
    gather x2 -> x0, local copies, waits for them, and re-layouts: 11.2 us -> none  [the longest x1 9.94 us: local(): pair_signal = jnp.take(everything, chosen, axis=0)]
  transfers between devices with their start and end apart: 2 -> 0, of which waited for: 2 -> 0; matrix products, arithmetic and copies ran while one was open for 13% -> 0% of each run, Pallas kernels for 0% -> 0%
where the time goes in v1:
time: 44 us; the launch traced here: 43.7 us
  Pallas kernels  37.6 us (85%)
  local copies, waits for them, and re-layouts  5.47 us (12%)
  between operations  0.7 us (2%)
    pallas_call x1, Pallas kernels, local(): pl.pallas_call(functools.partial(kernel, n, nd, taps), out_shape=jax.Shap...  37.6 us
    unnamed x19, local copies, waits for them, and re-layouts  5.47 us

profile of v1, /device:TPU:1, one launch (start us, length us, event | category | flops | bytes accessed | tf_op | source)
XLA Modules:
  0.0 43.7 jit_solution(18438265740411735149)
XLA Ops:
  0.7 0.0 copy-start.7
  0.7 0.0 copy-start.8
  0.7 0.0 copy-start.5
  0.7 0.0 copy-start.6
  0.7 0.6 %copy-done.7 = s32[128]{0:T(128)S(1)} copy-done((s32[128]{0:T(128)S(1)}, s32[128]{0:T(128)}, u32[]{:S(2)}) %copy-start.7) | copy-done | bytes 536
  1.3 0.0 copy-done.8
  1.3 0.0 copy-done.5
  1.4 0.0 copy-done.6
  1.4 0.0 copy-start
  1.4 0.9 %copy-done = bf16[256,256]{1,0:T(8,128)(2,1)S(1)} copy-done((bf16[256,256]{1,0:T(8,128)(2,1)S(1)}, bf16[256,256]{1,0:T(8,128)(2,1)}, u32[]{:S(2)}) %copy-start) | copy-done | bytes 131096
  2.3 0.0 copy-start.1
  2.3 0.9 %copy-done.1 = bf16[4,64,256]{2,1,0:T(8,128)(2,1)S(1)} copy-done((bf16[4,64,256]{2,1,0:T(8,128)(2,1)S(1)}, bf16[4,64,256]{2,1,0:T(8,128)(2,1)}, u32[]{:S(2)}) %copy-start.1) | copy-done | bytes 131096
  3.2 0.0 copy-start.2
  3.2 0.8 %copy-done.2 = bf16[256,128]{1,0:T(8,128)(2,1)S(1)} copy-done((bf16[256,128]{1,0:T(8,128)(2,1)S(1)}, bf16[256,128]{1,0:T(8,128)(2,1)}, u32[]{:S(2)}) %copy-start.2) | copy-done | bytes 65560
  4.0 0.0 copy-start.3
  4.0 0.8 %copy-done.3 = s32[64,64]{1,0:T(8,128)S(1)} copy-done((s32[64,64]{1,0:T(8,128)S(1)}, s32[64,64]{1,0:T(8,128)}, u32[]{:S(2)}) %copy-start.3) | copy-done | bytes 16408
  4.8 0.0 copy-start.4
  4.8 0.8 %copy-done.4 = s32[64,64]{1,0:T(8,128)S(1)} copy-done((s32[64,64]{1,0:T(8,128)S(1)}, s32[64,64]{1,0:T(8,128)}, u32[]{:S(2)}) %copy-start.4) | copy-done | bytes 16408
  5.5 37.6 %far_field.1 = bf16[4,64,128]{2,1,0:T(8,128)(2,1)S(1)} custom-call(bf16[256,128]{1,0:T(8,128)(2,1)S(1)} %copy-done.2, s32[1,256]{1,0:T(1,128)S(1)} %bitcast.10, bf16[256,256]{1,0:T(8,128)(2,1)S(1)} %copy-done, bf16[256,256]{1,0:T(8,128)(2,1)S(1)} %bitcast.9, s32[1,128]{1,0:T(1,128)S(1)} %bitcast.11, s32[1,128]{1,0:T(1,128)S(1)} %bitcast.12, ...), custom_call_target="tpu_custom_call" | custom-call | tf_op jit(solution)/shard_map/far_field/pallas_call | solution.py:325
  43.1 0.6 %copy.13 = bf16[256,128]{1,0:T(8,128)(2,1)} copy(bf16[256,128]{1,0:T(8,128)(2,1)S(1)} %bitcast.8) | data formatting | bytes 131072
Async XLA Ops:
  0.7 0.7 %copy-start.7 = (s32[128]{0:T(128)S(1)}, s32[128]{0:T(128)}, u32[]{:S(2)}) copy-start(s32[128]{0:T(128)} %param.15) | copy-start | bytes 1540
  0.7 0.7 %copy-start.8 = (s32[128]{0:T(128)S(1)}, s32[128]{0:T(128)}, u32[]{:S(2)}) copy-start(s32[128]{0:T(128)} %param.16) | copy-start | bytes 1540
  0.7 0.7 %copy-start.5 = (s32[256]{0:T(256)S(1)}, s32[256]{0:T(256)}, u32[]{:S(2)}) copy-start(s32[256]{0:T(256)} %param.11) | copy-start | bytes 3076
  0.7 0.7 %copy-start.6 = (s32[128]{0:T(128)S(1)}, s32[128]{0:T(128)}, u32[]{:S(2)}) copy-start(s32[128]{0:T(128)} %param.14) | copy-start | bytes 1540
  1.4 0.9 %copy-start = (bf16[256,256]{1,0:T(8,128)(2,1)S(1)}, bf16[256,256]{1,0:T(8,128)(2,1)}, u32[]{:S(2)}) copy-start(bf16[256,256]{1,0:T(8,128)(2,1)} %proj_h.1) | copy-start | bytes 393220
  2.3 0.9 %copy-start.1 = (bf16[4,64,256]{2,1,0:T(8,128)(2,1)S(1)}, bf16[4,64,256]{2,1,0:T(8,128)(2,1)}, u32[]{:S(2)}) copy-start(bf16[4,64,256]{2,1,0:T(8,128)(2,1)} %param.13) | copy-start | bytes 393220
  3.2 0.8 %copy-start.2 = (bf16[256,128]{1,0:T(8,128)(2,1)S(1)}, bf16[256,128]{1,0:T(8,128)(2,1)}, u32[]{:S(2)}) copy-start(bf16[256,128]{1,0:T(8,128)(2,1)} %cur_h.1) | copy-start | bytes 196612
  4.0 0.8 %copy-start.3 = (s32[64,64]{1,0:T(8,128)S(1)}, s32[64,64]{1,0:T(8,128)}, u32[]{:S(2)}) copy-start(s32[64,64]{1,0:T(8,128)} %sg_h.1) | copy-start | bytes 49156
  4.8 0.8 %copy-start.4 = (s32[64,64]{1,0:T(8,128)S(1)}, s32[64,64]{1,0:T(8,128)}, u32[]{:S(2)}) copy-start(s32[64,64]{1,0:T(8,128)} %rg_h.1) | copy-start | bytes 49156

commit v2 on v1

v2 whole, which is shorter than its diff:
```python
import functools

import jax
import jax.numpy as jnp
from jax import lax
from jax.experimental import pallas as pl
from jax.experimental.pallas import tpu as pltpu
from jax.sharding import PartitionSpec as P

MESH = pl.DeviceIdType.MESH
F32 = jnp.float32
BF16 = jnp.bfloat16
TYPES = 4
GROUPS_OWN = 2
HALVES = 1
KH = 4
ROWS = GROUPS_OWN * KH
NTAB = 4
READER_CHUNK = 8


def dot_nt(a, b):
    return lax.dot_general(a, b, (((1,), (1,)), ((), ())), preferred_element_type=F32)


def dot(a, b):
    return jnp.dot(a, b, preferred_element_type=F32)


def iota(shape, axis):
    return lax.broadcasted_iota(jnp.int32, shape, axis)


def kernel(
    n,
    nd,
    taps,
    cur_h,
    bg_h,
    proj_h,
    filt_h,
    src_h,
    dst_h,
    typ_h,
    live_h,
    sg_h,
    rg_h,
    out,
    cur,
    bg,
    proj,
    filt,
    src,
    dst,
    typ,
    live,
    sg,
    rg,
    local_sems,
    tab_send,
    tab_recv,
    sig_send,
    sig_recv,
    in_send,
    in_recv,
    term_send,
    term_recv,
    send_sems,
    recv_sems,
    pattern,
    back,
    toep,
    index_b,
    index_s,
    rows_f,
):
    p = lax.axis_index("grp")
    d = lax.axis_index("dir")
    rows, steps = cur.shape
    slots = src.shape[1]
    groups = GROUPS_OWN * n

    locals_ = []
    for i, (a, b) in enumerate(
        [
            (src_h, src),
            (dst_h, dst),
            (typ_h, typ),
            (live_h, live),
            (sg_h, sg),
            (rg_h, rg),
            (proj_h, proj),
            (cur_h, cur),
            (bg_h, bg),
            (filt_h, filt),
        ]
    ):
        copy = pltpu.make_async_copy(a, b, local_sems.at[i])
        copy.start()
        locals_.append(copy)

    barrier = pltpu.get_barrier_semaphore()

    def greet(i, carry):
        pl.semaphore_signal(barrier, 1, device_id=(lax.rem(p + i, n), d), device_id_type=MESH)
        return carry

    lax.fori_loop(1, n, greet, 0)
    for i in range(1, nd):
        pl.semaphore_signal(barrier, 1, device_id=(p, lax.rem(d + i, nd)), device_id_type=MESH)

    for copy in locals_[:6]:
        copy.wait()
    owners = iota((n, slots), 0)
    here = iota((n, n), 1) == p
    send_col = jnp.sum(jnp.where(here, sg[...].astype(F32), 0.0), axis=1, keepdims=True)
    recv_col = jnp.sum(jnp.where(here, rg[...].astype(F32), 0.0), axis=1, keepdims=True)
    send_of = jnp.sum(jnp.where(owners == src[...], send_col, 0.0), axis=0, keepdims=True)
    recv_of = jnp.sum(jnp.where(owners == dst[...], recv_col, 0.0), axis=0, keepdims=True)
    source = send_of * n + src[...].astype(F32)
    target = recv_of * n + dst[...].astype(F32)
    is_live = jnp.where(iota((1, slots), 1) < live[...], 1.0, 0.0)
    row = iota((NTAB, slots), 0)
    table = jnp.where(
        row == 0,
        source,
        jnp.where(row == 1, target, jnp.where(row == 2, typ[...].astype(F32), is_live)),
    )
    tab_send[...] = table.astype(BF16)
    tab_recv[pl.ds(p, 1)] = table.astype(BF16)[None]

    for copy in locals_[6:9]:
        copy.wait()
    width = proj.shape[1]
    pick = (iota((GROUPS_OWN * width, width), 0) // GROUPS_OWN == iota((GROUPS_OWN * width, width), 1))
    spread = dot_nt(pick.astype(F32).astype(BF16), proj[...])
    owned = lax.rem(iota((GROUPS_OWN * width, rows), 0), GROUPS_OWN) == bg[...]
    pattern[...] = jnp.where(owned, spread, 0.0).astype(BF16)
    signature = dot(pattern[...], cur[...])
    sig_send[...] = signature.reshape(HALVES, n, ROWS, steps).astype(BF16)
    for h in range(HALVES):
        sig_recv[h, pl.ds(p, 1)] = sig_send[h, pl.ds(p, 1)]

    pl.semaphore_wait(barrier, n - 1 + nd - 1)

    def to_peers(src_of, dst, sem):
        def send(i, carry):
            peer = lax.rem(p + i, n)
            pltpu.make_async_remote_copy(
                src_ref=src_of(peer),
                dst_ref=dst.at[p],
                send_sem=send_sems.at[sem],
                recv_sem=recv_sems.at[sem],
                device_id=(peer, d),
                device_id_type=MESH,
            ).start()
            return carry

        lax.fori_loop(1, n, send, 0)

    to_peers(lambda peer: tab_send, tab_recv, 0)
    for h in range(HALVES):
        to_peers(lambda peer, h=h: sig_send.at[h, peer], sig_recv.at[h], 1 + h)

    def await_bytes(ref, sem):
        pltpu.make_async_copy(ref, ref, sem).wait()

    eye = (iota((rows, rows), 0) == iota((rows, rows), 1)).astype(F32).astype(BF16)
    back[...] = dot_nt(eye, pattern[...]).astype(BF16)
    locals_[9].wait()
    unit = iota((8, width), 0)
    mine = (iota((8, width), 1) == unit // KH * (n * KH) + KH * p + lax.rem(unit, KH)) & (
        unit < HALVES * KH
    )
    tap_rows = dot_nt(mine.astype(F32).astype(BF16), filt[...])
    lag = iota((steps, steps), 1) - iota((steps, steps), 0)
    causal = (lag >= 0) & (lag < taps)
    for k in range(HALVES * KH):
        for c in range(TYPES):
            first = c * taps
            base = first // steps * steps
            line = jnp.broadcast_to(tap_rows[k : k + 1, base : base + steps], (steps, steps))
            turned = pltpu.roll(line, (steps - (first - base)) % steps, 1, stride=1, stride_axis=0)
            toep[k, c * steps : (c + 1) * steps, :] = jnp.where(causal, turned, 0.0).astype(BF16)

    await_bytes(tab_recv.at[pl.ds(0, n - 1)], recv_sems.at[0])
    tables = tab_recv[...].astype(F32)
    kind = tables[:, 2, :]
    high = jnp.where(kind >= 2.0, 1.0, 0.0)
    index_b[...] = jnp.where(tables[:, 3, :] > 0.0, high * groups + tables[:, 1, :], -1.0)
    index_s[...] = (kind - 2.0 * high) * groups + tables[:, 0, :]
    wide = iota((2 * groups, slots), 0).astype(F32)

    def count_readers(step, total):
        hot_b, hot_s = [], []
        for j in range(READER_CHUNK):
            r = step * READER_CHUNK + j
            hot_b.append(jnp.where(wide == index_b[pl.ds(r, 1), :], 1.0, 0.0).astype(BF16))
            hot_s.append(jnp.where(wide == index_s[pl.ds(r, 1), :], 1.0, 0.0).astype(BF16))
        return total + dot_nt(jnp.concatenate(hot_b, axis=1), jnp.concatenate(hot_s, axis=1))

    count = lax.fori_loop(
        0, n // READER_CHUNK, count_readers, jnp.zeros((2 * groups, 2 * groups), F32)
    )
    hundreds = jnp.floor(count * (1.0 / 256.0))
    units = count - 256.0 * hundreds
    parts = []
    for c in range(TYPES):
        r0, c0 = c // 2 * groups, c % 2 * groups
        parts.append(
            jnp.concatenate(
                [
                    units[r0 : r0 + groups, c0 : c0 + groups],
                    hundreds[r0 : r0 + groups, c0 : c0 + groups],
                ],
                axis=1,
            )
        )
    counts = jnp.concatenate(parts, axis=0).astype(BF16)

    for h in range(HALVES):
        await_bytes(sig_recv.at[h, pl.ds(0, n - 1)], recv_sems.at[1 + h])
        rows_f[...] = sig_recv[h].astype(F32)
        by_k = []
        for k in range(KH):
            by_k.append(
                jnp.concatenate([rows_f[:, GROUPS_OWN * k + g, :] for g in range(GROUPS_OWN)], axis=0)
            )
        signal = jnp.concatenate(by_k, axis=1)
        signal = jnp.concatenate([signal, 256.0 * signal], axis=0).astype(BF16)
        summed = dot(counts, signal)
        for k in range(KH):
            part = summed[:, k * steps : (k + 1) * steps]
            part = jnp.concatenate([part[c * groups : (c + 1) * groups] for c in range(TYPES)], axis=1)
            upper = part.astype(BF16)
            lower = (part - upper.astype(F32)).astype(BF16)
            both = dot(jnp.concatenate([upper, lower], axis=0), toep[KH * h + k])
            arriving = both[:groups] + both[groups:]
            for g in range(GROUPS_OWN):
                rows_f[:, GROUPS_OWN * k + g, :] = arriving[g * n : (g + 1) * n]
        in_send[h] = rows_f[...].astype(BF16)
        in_recv[h, pl.ds(p, 1)] = in_send[h, pl.ds(p, 1)]
        to_peers(lambda peer, h=h: in_send.at[h, peer], in_recv.at[h], 3 + h)

    total = jnp.zeros((rows, steps), F32)
    for h in range(HALVES):
        await_bytes(in_recv.at[h, pl.ds(0, n - 1)], recv_sems.at[3 + h])
        incoming = in_recv[h].astype(F32).reshape(n * ROWS, steps).astype(BF16)
        total = total + dot(back[:, h * n * ROWS : (h + 1) * n * ROWS], incoming)
    term_send[...] = total.astype(BF16)
    for i in range(1, nd):
        pltpu.make_async_remote_copy(
            src_ref=term_send,
            dst_ref=term_recv.at[d],
            send_sem=send_sems.at[5],
            recv_sem=recv_sems.at[5],
            device_id=(p, lax.rem(d + i, nd)),
            device_id_type=MESH,
        ).start()
    term_recv[pl.ds(d, 1)] = term_send[...][None]
    await_bytes(tab_recv.at[pl.ds(0, n - 1)], send_sems.at[0])
    for h in range(HALVES):
        await_bytes(sig_send.at[h, pl.ds(0, n - 1)], send_sems.at[1 + h])
        await_bytes(in_send.at[h, pl.ds(0, n - 1)], send_sems.at[3 + h])
    await_bytes(term_recv.at[pl.ds(0, nd - 1)], recv_sems.at[5])
    field = term_recv[0].astype(F32)
    for i in range(1, nd):
        field = field + term_recv[i].astype(F32)
    out[...] = field.astype(BF16)
    await_bytes(term_recv.at[pl.ds(0, nd - 1)], send_sems.at[5])


def local(
    currents,
    basis_group,
    projection,
    filters,
    pair_src,
    pair_dst,
    pair_type,
    live_count,
    send_group,
    recv_group,
):
    n = lax.axis_size("grp")
    nd = lax.axis_size("dir")
    rows, steps = currents.shape
    width = projection.shape[1]
    taps = filters.shape[1]
    slots = pair_src.shape[0]
    groups = GROUPS_OWN * n
    any_space = pl.BlockSpec(memory_space=pltpu.HBM)
    return pl.pallas_call(
        functools.partial(kernel, n, nd, taps),
        out_shape=pltpu.VMEM((rows, steps), BF16),
        in_specs=[any_space] * 10,
        out_specs=pl.BlockSpec(memory_space=pltpu.VMEM),
        scratch_shapes=[
            pltpu.VMEM((rows, steps), BF16),
            pltpu.VMEM((1, rows), jnp.int32),
            pltpu.VMEM((rows, width), BF16),
            pltpu.VMEM((TYPES * taps, width), BF16),
            pltpu.VMEM((1, slots), jnp.int32),
            pltpu.VMEM((1, slots), jnp.int32),
            pltpu.VMEM((1, slots), jnp.int32),
            pltpu.VMEM((1, 1), jnp.int32),
            pltpu.VMEM((n, n), jnp.int32),
            pltpu.VMEM((n, n), jnp.int32),
            pltpu.SemaphoreType.DMA((10,)),
            pltpu.VMEM((NTAB, slots), BF16),
            pltpu.VMEM((n, NTAB, slots), BF16),
            pltpu.VMEM((HALVES, n, ROWS, steps), BF16),
            pltpu.VMEM((HALVES, n, ROWS, steps), BF16),
            pltpu.VMEM((HALVES, n, ROWS, steps), BF16),
            pltpu.VMEM((HALVES, n, ROWS, steps), BF16),
            pltpu.VMEM((rows, steps), BF16),
            pltpu.VMEM((nd, rows, steps), BF16),
            pltpu.SemaphoreType.DMA((6,)),
            pltpu.SemaphoreType.DMA((6,)),
            pltpu.VMEM((GROUPS_OWN * width, rows), BF16),
            pltpu.VMEM((rows, GROUPS_OWN * width), BF16),
            pltpu.VMEM((HALVES * KH, TYPES * steps, steps), BF16),
            pltpu.VMEM((n, slots), F32),
            pltpu.VMEM((n, slots), F32),
            pltpu.VMEM((n, ROWS, steps), F32),
        ],
        compiler_params=pltpu.CompilerParams(
            collective_id=0, has_side_effects=True, vmem_limit_bytes=63 * 1024 * 1024
        ),
        name="far_field",
    )(
        currents,
        basis_group.reshape(1, rows),
        projection,
        filters.reshape(TYPES * taps, width),
        pair_src.reshape(1, slots),
        pair_dst.reshape(1, slots),
        pair_type.reshape(1, slots),
        live_count.reshape(1, 1),
        send_group,
        recv_group,
    )


def solution(mesh):
    return jax.shard_map(
        local,
        mesh=mesh,
        in_specs=(
            P("grp", None),
            P("grp"),
            P("grp", "dir"),
            P(None, None, "dir"),
            P("grp"),
            P("grp"),
            P("grp"),
            P("grp"),
            P(),
            P(),
        ),
        out_specs=P("grp", None),
        check_vma=False,
    )
```

time: 44 us -> 37.2 us (0.85)
  local copies, waits for them, and re-layouts: 5.47 us -> 0.63 us
  Pallas kernels: 37.6 us -> 35.8 us
    unnamed x19 -> x1, local copies, waits for them, and re-layouts: 5.47 us -> 0.63 us
    pallas_call x1, Pallas kernels: 37.6 us -> 35.8 us  [local(): pl.pallas_call(functools.partial(kernel, n, nd, taps), out_shape=pltpu.VM...]
where the time goes in v2:
time: 37.2 us; the launch traced here: 37.1 us
  Pallas kernels  35.8 us (96%)
  between operations  0.66 us (2%)
  local copies, waits for them, and re-layouts  0.63 us (2%)
    pallas_call x1, Pallas kernels, local(): pl.pallas_call(functools.partial(kernel, n, nd, taps), out_shape=pltpu.VM...  35.8 us

profile of v2, /device:TPU:1, one launch (start us, length us, event | category | flops | bytes accessed | tf_op | source)
XLA Modules:
  0.0 37.1 jit_solution(1381499389315720430)
XLA Ops:
  0.7 35.8 %far_field.1 = bf16[256,128]{1,0:T(8,128)(2,1)S(1)} custom-call(bf16[256,128]{1,0:T(8,128)(2,1)} %cur_h.1, s32[1,256]{1,0:T(1,128)} %bitcast.8, bf16[256,256]{1,0:T(8,128)(2,1)} %proj_h.1, bf16[256,256]{1,0:T(8,128)(2,1)} %bitcast.7, s32[1,128]{1,0:T(1,128)} %bitcast.9, s32[1,128]{1,0:T(1,128)} %bitcast.10, s32[1,128]{1,0:T(1,128)} %bitcast.11, ...), custom_call_target="tpu_custom_call" | custom-call | tf_op jit(solution)/shard_map/far_field/pallas_call | solution.py:293
  36.5 0.6 %copy.12 = bf16[256,128]{1,0:T(8,128)(2,1)} copy(bf16[256,128]{1,0:T(8,128)(2,1)S(1)} %far_field.1) | data formatting | bytes 131072

commit v3 on v2

--- a/solution.py
+++ b/solution.py
@@ -12,11 +12,11 @@
 BF16 = jnp.bfloat16
 TYPES = 4
 GROUPS_OWN = 2
-HALVES = 1
-KH = 4
+HALVES = 2
+KH = 2
 ROWS = GROUPS_OWN * KH
 NTAB = 4
-READER_CHUNK = 8
+BLOCK = 16
 
 
 def dot_nt(a, b):
@@ -67,11 +67,10 @@
     term_recv,
     send_sems,
     recv_sems,
+    table_sems,
     pattern,
     back,
     toep,
-    index_b,
-    index_s,
     rows_f,
 ):
     p = lax.axis_index("grp")
@@ -79,6 +78,33 @@
     rows, steps = cur.shape
     slots = src.shape[1]
     groups = GROUPS_OWN * n
+
+    block = min(BLOCK, n)
+    half = block // 2
+    lane = p & (block - 1)
+    late = jnp.where(lane < half, 0, 1)
+    ys = n // block
+    z = lane >> 1
+    across = [
+        (((p // block + r // 2) & (ys - 1)) * block) | ((lane & 1) ^ (r & 1)) for r in range(2 * ys)
+    ]
+
+    def each_peer(act):
+        def step(u, carry):
+            away = half // 2 + jnp.where((u & 1) == 1, (u + 1) >> 1, half - (u >> 1))
+            place = ((z + away) & (half - 1)) << 1
+            for base in across:
+                act(base | place)
+            return carry
+
+        lax.fori_loop(0, half - 1, step, 0)
+        for base in across[1:]:
+            act(base | (z << 1))
+
+    barrier = pltpu.get_barrier_semaphore()
+    each_peer(lambda peer: pl.semaphore_signal(barrier, 1, device_id=(peer, d), device_id_type=MESH))
+    for i in range(1, nd):
+        pl.semaphore_signal(barrier, 1, device_id=(p, lax.rem(d + i, nd)), device_id_type=MESH)
 
     locals_ = []
     for i, (a, b) in enumerate(
@@ -98,16 +124,6 @@
         copy = pltpu.make_async_copy(a, b, local_sems.at[i])
         copy.start()
         locals_.append(copy)
-
-    barrier = pltpu.get_barrier_semaphore()
-
-    def greet(i, carry):
-        pl.semaphore_signal(barrier, 1, device_id=(lax.rem(p + i, n), d), device_id_type=MESH)
-        return carry
-
-    lax.fori_loop(1, n, greet, 0)
-    for i in range(1, nd):
-        pl.semaphore_signal(barrier, 1, device_id=(p, lax.rem(d + i, nd)), device_id_type=MESH)
 
     for copy in locals_[:6]:
         copy.wait()
@@ -143,24 +159,22 @@
 
     pl.semaphore_wait(barrier, n - 1 + nd - 1)
 
-    def to_peers(src_of, dst, sem):
-        def send(i, carry):
-            peer = lax.rem(p + i, n)
+    def to_peers(src_of, dst, sem, recv_sem):
+        def send(peer):
             pltpu.make_async_remote_copy(
                 src_ref=src_of(peer),
                 dst_ref=dst.at[p],
                 send_sem=send_sems.at[sem],
-                recv_sem=recv_sems.at[sem],
+                recv_sem=recv_sem,
                 device_id=(peer, d),
                 device_id_type=MESH,
             ).start()
-            return carry
-
-        lax.fori_loop(1, n, send, 0)
-
-    to_peers(lambda peer: tab_send, tab_recv, 0)
-    for h in range(HALVES):
-        to_peers(lambda peer, h=h: sig_send.at[h, peer], sig_recv.at[h], 1 + h)
+
+        each_peer(send)
+
+    to_peers(lambda peer: tab_send, tab_recv, 0, table_sems.at[late])
+    for h in range(HALVES):
+        to_peers(lambda peer, h=h: sig_send.at[h, peer], sig_recv.at[h], 1 + h, recv_sems.at[1 + h])
 
     def await_bytes(ref, sem):
         pltpu.make_async_copy(ref, ref, sem).wait()
@@ -183,25 +197,36 @@
             turned = pltpu.roll(line, (steps - (first - base)) % steps, 1, stride=1, stride_axis=0)
             toep[k, c * steps : (c + 1) * steps, :] = jnp.where(causal, turned, 0.0).astype(BF16)
 
-    await_bytes(tab_recv.at[pl.ds(0, n - 1)], recv_sems.at[0])
-    tables = tab_recv[...].astype(F32)
-    kind = tables[:, 2, :]
-    high = jnp.where(kind >= 2.0, 1.0, 0.0)
-    index_b[...] = jnp.where(tables[:, 3, :] > 0.0, high * groups + tables[:, 1, :], -1.0)
-    index_s[...] = (kind - 2.0 * high) * groups + tables[:, 0, :]
-    wide = iota((2 * groups, slots), 0).astype(F32)
-
-    def count_readers(step, total):
-        hot_b, hot_s = [], []
-        for j in range(READER_CHUNK):
-            r = step * READER_CHUNK + j
-            hot_b.append(jnp.where(wide == index_b[pl.ds(r, 1), :], 1.0, 0.0).astype(BF16))
-            hot_s.append(jnp.where(wide == index_s[pl.ds(r, 1), :], 1.0, 0.0).astype(BF16))
-        return total + dot_nt(jnp.concatenate(hot_b, axis=1), jnp.concatenate(hot_s, axis=1))
-
-    count = lax.fori_loop(
-        0, n // READER_CHUNK, count_readers, jnp.zeros((2 * groups, 2 * groups), F32)
-    )
+    wide = iota((2 * groups, slots), 0).astype(F32).astype(BF16)
+    one, none = jnp.ones((), BF16), jnp.zeros((), BF16)
+
+    def hot(index):
+        spread = jnp.broadcast_to(index, (2 * groups, slots)).astype(BF16)
+        return jnp.where(wide == spread, one, none)
+
+    count = jnp.zeros((2 * groups, 2 * groups), F32)
+    for part in (1, 0):
+
+        @pl.when(late == part)
+        def _():
+            await_bytes(tab_recv.at[pl.ds(0, n // 2 - 1)], table_sems.at[part])
+
+        @pl.when(late != part)
+        def _():
+            await_bytes(tab_recv.at[pl.ds(0, n // 2)], table_sems.at[part])
+
+        def count_block(y, total):
+            readers = pl.ds(y * block + half * part, half)
+            tables = tab_recv[readers].astype(F32)
+            kind = tables[:, 2, :]
+            high = jnp.where(kind >= 2.0, 1.0, 0.0)
+            index_b = jnp.where(tables[:, 3, :] > 0.0, high * groups + tables[:, 1, :], -1.0)
+            index_s = (kind - 2.0 * high) * groups + tables[:, 0, :]
+            hot_b = [hot(index_b[j : j + 1]) for j in range(half)]
+            hot_s = [hot(index_s[j : j + 1]) for j in range(half)]
+            return total + dot_nt(jnp.concatenate(hot_b, axis=1), jnp.concatenate(hot_s, axis=1))
+
+        count = lax.fori_loop(0, n // block, count_block, count)
     hundreds = jnp.floor(count * (1.0 / 256.0))
     units = count - 256.0 * hundreds
     parts = []
@@ -240,34 +265,37 @@
                 rows_f[:, GROUPS_OWN * k + g, :] = arriving[g * n : (g + 1) * n]
         in_send[h] = rows_f[...].astype(BF16)
         in_recv[h, pl.ds(p, 1)] = in_send[h, pl.ds(p, 1)]
-        to_peers(lambda peer, h=h: in_send.at[h, peer], in_recv.at[h], 3 + h)
-
-    total = jnp.zeros((rows, steps), F32)
+        to_peers(lambda peer, h=h: in_send.at[h, peer], in_recv.at[h], 3 + h, recv_sems.at[3 + h])
+
+    incoming = []
     for h in range(HALVES):
         await_bytes(in_recv.at[h, pl.ds(0, n - 1)], recv_sems.at[3 + h])
-        incoming = in_recv[h].astype(F32).reshape(n * ROWS, steps).astype(BF16)
-        total = total + dot(back[:, h * n * ROWS : (h + 1) * n * ROWS], incoming)
-    term_send[...] = total.astype(BF16)
-    for i in range(1, nd):
-        pltpu.make_async_remote_copy(
-            src_ref=term_send,
-            dst_ref=term_recv.at[d],
-            send_sem=send_sems.at[5],
-            recv_sem=recv_sems.at[5],
-            device_id=(p, lax.rem(d + i, nd)),
-            device_id_type=MESH,
-        ).start()
-    term_recv[pl.ds(d, 1)] = term_send[...][None]
+        incoming.append(in_recv[h].astype(F32).reshape(n * ROWS, steps).astype(BF16))
+    incoming = jnp.concatenate(incoming, axis=0)
+    part = rows // 2
+    for b in range(2):
+        term_send[b] = dot(back[b * part : (b + 1) * part], incoming).astype(BF16)
+        for i in (2, 1, 3) if nd == 4 else range(1, nd):
+            pltpu.make_async_remote_copy(
+                src_ref=term_send.at[b],
+                dst_ref=term_recv.at[b, d],
+                send_sem=send_sems.at[5 + b],
+                recv_sem=recv_sems.at[5 + b],
+                device_id=(p, lax.rem(d + i, nd)),
+                device_id_type=MESH,
+            ).start()
+        term_recv[b, pl.ds(d, 1)] = term_send[b][None]
     await_bytes(tab_recv.at[pl.ds(0, n - 1)], send_sems.at[0])
     for h in range(HALVES):
         await_bytes(sig_send.at[h, pl.ds(0, n - 1)], send_sems.at[1 + h])
         await_bytes(in_send.at[h, pl.ds(0, n - 1)], send_sems.at[3 + h])
-    await_bytes(term_recv.at[pl.ds(0, nd - 1)], recv_sems.at[5])
-    field = term_recv[0].astype(F32)
-    for i in range(1, nd):
-        field = field + term_recv[i].astype(F32)
-    out[...] = field.astype(BF16)
-    await_bytes(term_recv.at[pl.ds(0, nd - 1)], send_sems.at[5])
+    for b in range(2):
+        await_bytes(term_recv.at[b, pl.ds(0, nd - 1)], recv_sems.at[5 + b])
+        field = term_recv[b, 0].astype(F32)
+        for i in range(1, nd):
+            field = field + term_recv[b, i].astype(F32)
+        out[b * part : (b + 1) * part, :] = field.astype(BF16)
+        await_bytes(term_recv.at[b, pl.ds(0, nd - 1)], send_sems.at[5 + b])
 
 
 def local(
@@ -313,15 +341,14 @@
             pltpu.VMEM((HALVES, n, ROWS, steps), BF16),
             pltpu.VMEM((HALVES, n, ROWS, steps), BF16),
             pltpu.VMEM((HALVES, n, ROWS, steps), BF16),
-            pltpu.VMEM((rows, steps), BF16),
-            pltpu.VMEM((nd, rows, steps), BF16),
-            pltpu.SemaphoreType.DMA((6,)),
-            pltpu.SemaphoreType.DMA((6,)),
+            pltpu.VMEM((2, rows // 2, steps), BF16),
+            pltpu.VMEM((2, nd, rows // 2, steps), BF16),
+            pltpu.SemaphoreType.DMA((7,)),
+            pltpu.SemaphoreType.DMA((7,)),
+            pltpu.SemaphoreType.DMA((2,)),
             pltpu.VMEM((GROUPS_OWN * width, rows), BF16),
             pltpu.VMEM((rows, GROUPS_OWN * width), BF16),
             pltpu.VMEM((HALVES * KH, TYPES * steps, steps), BF16),
-            pltpu.VMEM((n, slots), F32),
-            pltpu.VMEM((n, slots), F32),
             pltpu.VMEM((n, ROWS, steps), F32),
         ],
         compiler_params=pltpu.CompilerParams(

time: 37.2 us -> 33.8 us (0.909)
  Pallas kernels: 35.8 us -> 32.4 us
    pallas_call x1, Pallas kernels: 35.8 us -> 32.4 us  [local(): pl.pallas_call(functools.partial(kernel, n, nd, taps), out_shape=pltpu.VM...]
where the time goes in v3:
time: 33.8 us; the launch traced here: 33.7 us
  Pallas kernels  32.4 us (96%)
  between operations  0.66 us (2%)
  local copies, waits for them, and re-layouts  0.63 us (2%)
    pallas_call x1, Pallas kernels, local(): pl.pallas_call(functools.partial(kernel, n, nd, taps), out_shape=pltpu.VM...  32.4 us

profile of v3, /device:TPU:1, one launch (start us, length us, event | category | flops | bytes accessed | tf_op | source)
XLA Modules:
  0.0 33.7 jit_solution(16790419330812787271)
XLA Ops:
  0.7 32.4 %far_field.1 = bf16[256,128]{1,0:T(8,128)(2,1)S(1)} custom-call(bf16[256,128]{1,0:T(8,128)(2,1)} %cur_h.1, s32[1,256]{1,0:T(1,128)} %bitcast.8, bf16[256,256]{1,0:T(8,128)(2,1)} %proj_h.1, bf16[256,256]{1,0:T(8,128)(2,1)} %bitcast.7, s32[1,128]{1,0:T(1,128)} %bitcast.9, s32[1,128]{1,0:T(1,128)} %bitcast.10, s32[1,128]{1,0:T(1,128)} %bitcast.11, ...), custom_call_target="tpu_custom_call" | custom-call | tf_op jit(solution)/shard_map/far_field/pallas_call | solution.py:321
  33.1 0.6 %copy.12 = bf16[256,128]{1,0:T(8,128)(2,1)} copy(bf16[256,128]{1,0:T(8,128)(2,1)S(1)} %far_field.1) | data formatting | bytes 131072

commit v4 on v3

--- a/solution.py
+++ b/solution.py
@@ -90,16 +90,13 @@
     ]
 
     def each_peer(act):
-        def step(u, carry):
-            away = half // 2 + jnp.where((u & 1) == 1, (u + 1) >> 1, half - (u >> 1))
-            place = ((z + away) & (half - 1)) << 1
-            for base in across:
-                act(base | place)
-            return carry
-
-        lax.fori_loop(0, half - 1, step, 0)
-        for base in across[1:]:
-            act(base | (z << 1))
+        zs = [((z + i) & (half - 1)) << 1 for i in range(half)]
+        offs = [(a, r) for a in range(half) for r in range(2 * ys)][1:]
+        zd = lambda a: min(a, half - a)
+        yd = lambda r: min(r // 2, ys - r // 2)
+        offs.sort(key=lambda t: -(zd(t[0]) + yd(t[1])))
+        for a, r in offs:
+            act(across[r] | zs[a])
 
     barrier = pltpu.get_barrier_semaphore()
     each_peer(lambda peer: pl.semaphore_signal(barrier, 1, device_id=(peer, d), device_id_type=MESH))
@@ -153,8 +150,12 @@
     owned = lax.rem(iota((GROUPS_OWN * width, rows), 0), GROUPS_OWN) == bg[...]
     pattern[...] = jnp.where(owned, spread, 0.0).astype(BF16)
     signature = dot(pattern[...], cur[...])
-    sig_send[...] = signature.reshape(HALVES, n, ROWS, steps).astype(BF16)
-    for h in range(HALVES):
+    split = steps // 2
+    low, high = signature[: n * ROWS], signature[n * ROWS :]
+    for h in range(HALVES):
+        span = slice(h * split, (h + 1) * split)
+        packed = jnp.concatenate([low[:, span], high[:, span]], axis=1)
+        sig_send[h] = packed.reshape(n, ROWS, steps).astype(BF16)
         sig_recv[h, pl.ds(p, 1)] = sig_send[h, pl.ds(p, 1)]
 
     pl.semaphore_wait(barrier, n - 1 + nd - 1)
@@ -187,15 +188,23 @@
         unit < HALVES * KH
     )
     tap_rows = dot_nt(mine.astype(F32).astype(BF16), filt[...])
-    lag = iota((steps, steps), 1) - iota((steps, steps), 0)
+    lag = iota((split, steps), 1) - iota((split, steps), 0)
     causal = (lag >= 0) & (lag < taps)
-    for k in range(HALVES * KH):
+    left = iota((split, steps), 1) < split
+    for unit in range(HALVES * KH):
+        side, k = unit // KH, unit % KH
         for c in range(TYPES):
             first = c * taps
             base = first // steps * steps
-            line = jnp.broadcast_to(tap_rows[k : k + 1, base : base + steps], (steps, steps))
+            line = jnp.broadcast_to(tap_rows[unit : unit + 1, base : base + steps], (split, steps))
             turned = pltpu.roll(line, (steps - (first - base)) % steps, 1, stride=1, stride_axis=0)
-            toep[k, c * steps : (c + 1) * steps, :] = jnp.where(causal, turned, 0.0).astype(BF16)
+            wide = jnp.where(causal, turned, 0.0)
+            crossed = pltpu.roll(wide, split, 1)
+            here = left if side == 0 else jnp.logical_not(left)
+            same, next_half = (wide, crossed) if side == 0 else (crossed, wide)
+            at = pl.ds(c * steps + side * split, split)
+            toep[k, at, :] = jnp.where(here, same, 0.0).astype(BF16)
+            toep[KH + k, at, :] = jnp.where(here, next_half, 0.0).astype(BF16)
 
     wide = iota((2 * groups, slots), 0).astype(F32).astype(BF16)
     one, none = jnp.ones((), BF16), jnp.zeros((), BF16)
@@ -243,6 +252,7 @@
         )
     counts = jnp.concatenate(parts, axis=0).astype(BF16)
 
+    earlier = []
     for h in range(HALVES):
         await_bytes(sig_recv.at[h, pl.ds(0, n - 1)], recv_sems.at[1 + h])
         rows_f[...] = sig_recv[h].astype(F32)
@@ -259,7 +269,12 @@
             part = jnp.concatenate([part[c * groups : (c + 1) * groups] for c in range(TYPES)], axis=1)
             upper = part.astype(BF16)
             lower = (part - upper.astype(F32)).astype(BF16)
-            both = dot(jnp.concatenate([upper, lower], axis=0), toep[KH * h + k])
+            parts = jnp.concatenate([upper, lower], axis=0)
+            both = dot(parts, toep[k])
+            if h == 0:
+                earlier.append(parts)
+            else:
+                both = both + dot(earlier[k], toep[KH + k])
             arriving = both[:groups] + both[groups:]
             for g in range(GROUPS_OWN):
                 rows_f[:, GROUPS_OWN * k + g, :] = arriving[g * n : (g + 1) * n]
@@ -267,35 +282,40 @@
         in_recv[h, pl.ds(p, 1)] = in_send[h, pl.ds(p, 1)]
         to_peers(lambda peer, h=h: in_send.at[h, peer], in_recv.at[h], 3 + h, recv_sems.at[3 + h])
 
-    incoming = []
+    part = rows // 2
+    on_left = iota((part, steps), 1) < split
     for h in range(HALVES):
         await_bytes(in_recv.at[h, pl.ds(0, n - 1)], recv_sems.at[3 + h])
-        incoming.append(in_recv[h].astype(F32).reshape(n * ROWS, steps).astype(BF16))
-    incoming = jnp.concatenate(incoming, axis=0)
-    part = rows // 2
-    for b in range(2):
-        term_send[b] = dot(back[b * part : (b + 1) * part], incoming).astype(BF16)
+        incoming = in_recv[h].astype(F32).reshape(n * ROWS, steps).astype(BF16)
+        of_low = dot(back[:, : n * ROWS], incoming)
+        of_high = dot(back[:, n * ROWS :], incoming)
+        upper = of_low[:part] + pltpu.roll(of_high[:part], split, 1)
+        lower = pltpu.roll(of_low[part:], split, 1) + of_high[part:]
+        term_send[h] = jnp.where(on_left, upper, lower).astype(BF16)
         for i in (2, 1, 3) if nd == 4 else range(1, nd):
             pltpu.make_async_remote_copy(
-                src_ref=term_send.at[b],
-                dst_ref=term_recv.at[b, d],
-                send_sem=send_sems.at[5 + b],
-                recv_sem=recv_sems.at[5 + b],
+                src_ref=term_send.at[h],
+                dst_ref=term_recv.at[h, d],
+                send_sem=send_sems.at[5 + h],
+                recv_sem=recv_sems.at[5 + h],
                 device_id=(p, lax.rem(d + i, nd)),
                 device_id_type=MESH,
             ).start()
-        term_recv[b, pl.ds(d, 1)] = term_send[b][None]
+        term_recv[h, pl.ds(d, 1)] = term_send[h][None]
     await_bytes(tab_recv.at[pl.ds(0, n - 1)], send_sems.at[0])
     for h in range(HALVES):
         await_bytes(sig_send.at[h, pl.ds(0, n - 1)], send_sems.at[1 + h])
         await_bytes(in_send.at[h, pl.ds(0, n - 1)], send_sems.at[3 + h])
-    for b in range(2):
-        await_bytes(term_recv.at[b, pl.ds(0, nd - 1)], recv_sems.at[5 + b])
-        field = term_recv[b, 0].astype(F32)
+    fields = []
+    for h in range(HALVES):
+        await_bytes(term_recv.at[h, pl.ds(0, nd - 1)], recv_sems.at[5 + h])
+        field = term_recv[h, 0].astype(F32)
         for i in range(1, nd):
-            field = field + term_recv[b, i].astype(F32)
-        out[b * part : (b + 1) * part, :] = field.astype(BF16)
-        await_bytes(term_recv.at[b, pl.ds(0, nd - 1)], send_sems.at[5 + b])
+            field = field + term_recv[h, i].astype(F32)
+        fields.append(field)
+        await_bytes(term_recv.at[h, pl.ds(0, nd - 1)], send_sems.at[5 + h])
+    out[:part, :] = jnp.where(on_left, fields[0], pltpu.roll(fields[1], split, 1)).astype(BF16)
+    out[part:, :] = jnp.where(on_left, pltpu.roll(fields[0], split, 1), fields[1]).astype(BF16)
 
 
 def local(

time: 33.8 us -> 32.8 us (0.970)
  Pallas kernels: 32.4 us -> 31.4 us
    pallas_call x1, Pallas kernels: 32.4 us -> 31.4 us  [local(): pl.pallas_call(functools.partial(kernel, n, nd, taps), out_shape=pltpu.VM...]
where the time goes in v4:
time: 32.8 us; the launch traced here: 32.7 us
  Pallas kernels  31.4 us (96%)
  between operations  0.66 us (2%)
  local copies, waits for them, and re-layouts  0.63 us (2%)
    pallas_call x1, Pallas kernels, local(): pl.pallas_call(functools.partial(kernel, n, nd, taps), out_shape=pltpu.VM...  31.4 us

profile of v4, /device:TPU:1, one launch (start us, length us, event | category | flops | bytes accessed | tf_op | source)
XLA Modules:
  0.0 32.7 jit_solution(1243206536765804020)
XLA Ops:
  0.7 31.4 %far_field.1 = bf16[256,128]{1,0:T(8,128)(2,1)S(1)} custom-call(bf16[256,128]{1,0:T(8,128)(2,1)} %cur_h.1, s32[1,256]{1,0:T(1,128)} %bitcast.8, bf16[256,256]{1,0:T(8,128)(2,1)} %proj_h.1, bf16[256,256]{1,0:T(8,128)(2,1)} %bitcast.7, s32[1,128]{1,0:T(1,128)} %bitcast.9, s32[1,128]{1,0:T(1,128)} %bitcast.10, s32[1,128]{1,0:T(1,128)} %bitcast.11, ...), custom_call_target="tpu_custom_call" | custom-call | tf_op jit(solution)/shard_map/far_field/pallas_call | solution.py:341
  32.0 0.6 %copy.12 = bf16[256,128]{1,0:T(8,128)(2,1)} copy(bf16[256,128]{1,0:T(8,128)(2,1)S(1)} %far_field.1) | data formatting | bytes 131072

commit v5 on v4

--- a/solution.py
+++ b/solution.py
@@ -94,14 +94,9 @@
         offs = [(a, r) for a in range(half) for r in range(2 * ys)][1:]
         zd = lambda a: min(a, half - a)
         yd = lambda r: min(r // 2, ys - r // 2)
-        offs.sort(key=lambda t: -(zd(t[0]) + yd(t[1])))
+        offs.sort(key=lambda t: -(2 * zd(t[0]) + yd(t[1])))
         for a, r in offs:
             act(across[r] | zs[a])
-
-    barrier = pltpu.get_barrier_semaphore()
-    each_peer(lambda peer: pl.semaphore_signal(barrier, 1, device_id=(peer, d), device_id_type=MESH))
-    for i in range(1, nd):
-        pl.semaphore_signal(barrier, 1, device_id=(p, lax.rem(d + i, nd)), device_id_type=MESH)
 
     locals_ = []
     for i, (a, b) in enumerate(
@@ -121,6 +116,11 @@
         copy = pltpu.make_async_copy(a, b, local_sems.at[i])
         copy.start()
         locals_.append(copy)
+
+    barrier = pltpu.get_barrier_semaphore()
+    each_peer(lambda peer: pl.semaphore_signal(barrier, 1, device_id=(peer, d), device_id_type=MESH))
+    for i in range(1, nd):
+        pl.semaphore_signal(barrier, 1, device_id=(p, lax.rem(d + i, nd)), device_id_type=MESH)
 
     for copy in locals_[:6]:
         copy.wait()
@@ -302,10 +302,6 @@
                 device_id_type=MESH,
             ).start()
         term_recv[h, pl.ds(d, 1)] = term_send[h][None]
-    await_bytes(tab_recv.at[pl.ds(0, n - 1)], send_sems.at[0])
-    for h in range(HALVES):
-        await_bytes(sig_send.at[h, pl.ds(0, n - 1)], send_sems.at[1 + h])
-        await_bytes(in_send.at[h, pl.ds(0, n - 1)], send_sems.at[3 + h])
     fields = []
     for h in range(HALVES):
         await_bytes(term_recv.at[h, pl.ds(0, nd - 1)], recv_sems.at[5 + h])
@@ -313,9 +309,13 @@
         for i in range(1, nd):
             field = field + term_recv[h, i].astype(F32)
         fields.append(field)
-        await_bytes(term_recv.at[h, pl.ds(0, nd - 1)], send_sems.at[5 + h])
     out[:part, :] = jnp.where(on_left, fields[0], pltpu.roll(fields[1], split, 1)).astype(BF16)
     out[part:, :] = jnp.where(on_left, pltpu.roll(fields[0], split, 1), fields[1]).astype(BF16)
+    await_bytes(tab_recv.at[pl.ds(0, n - 1)], send_sems.at[0])
+    for h in range(HALVES):
+        await_bytes(sig_send.at[h, pl.ds(0, n - 1)], send_sems.at[1 + h])
+        await_bytes(in_send.at[h, pl.ds(0, n - 1)], send_sems.at[3 + h])
+        await_bytes(term_recv.at[h, pl.ds(0, nd - 1)], send_sems.at[5 + h])
 
 
 def local(

time: 32.8 us -> 32.6 us (level)
  no operation moved by 1% of the time
where the time goes in v5:
time: 32.6 us; the launch traced here: 32.5 us
  Pallas kernels  31.2 us (96%)
  between operations  0.66 us (2%)
  local copies, waits for them, and re-layouts  0.63 us (2%)
    pallas_call x1, Pallas kernels, local(): pl.pallas_call(functools.partial(kernel, n, nd, taps), out_shape=pltpu.VM...  31.2 us

profile of v5, /device:TPU:1, one launch (start us, length us, event | category | flops | bytes accessed | tf_op | source)
XLA Modules:
  0.0 32.5 jit_solution(12078728109803423523)
XLA Ops:
  0.7 31.2 %far_field.1 = bf16[256,128]{1,0:T(8,128)(2,1)S(1)} custom-call(bf16[256,128]{1,0:T(8,128)(2,1)} %cur_h.1, s32[1,256]{1,0:T(1,128)} %bitcast.8, bf16[256,256]{1,0:T(8,128)(2,1)} %proj_h.1, bf16[256,256]{1,0:T(8,128)(2,1)} %bitcast.7, s32[1,128]{1,0:T(1,128)} %bitcast.9, s32[1,128]{1,0:T(1,128)} %bitcast.10, s32[1,128]{1,0:T(1,128)} %bitcast.11, ...), custom_call_target="tpu_custom_call" | custom-call | tf_op jit(solution)/shard_map/far_field/pallas_call | solution.py:341
  31.9 0.6 %copy.12 = bf16[256,128]{1,0:T(8,128)(2,1)} copy(bf16[256,128]{1,0:T(8,128)(2,1)S(1)} %far_field.1) | data formatting | bytes 131072
